TPU v7x, 256 devices: a whole 4x4x8 slice. The times are simulated.
256 devices in a mesh: row: 8 (over y, x_hi), col: 32 (over x_lo, z, core).
Axes of the slice: x: 4 (x_hi: 2, x_lo: 2; x = x_hi * 2 + x_lo), y: 4, z: 8, core: 2. Of those that a mesh axis runs over, the one named last changes fastest.
Arguments:
- pair: bfloat16 [2560, 2560, 128], P('row', 'col'), may hold values from -6 to 6
- in_gain: float32 [128], replicated, may hold values from 0.1 to 1.9
- a_weight: bfloat16 [128, 256], replicated, may hold values from -0.5 to 0.5
- b_weight: bfloat16 [128, 256], replicated, may hold values from -0.5 to 0.5
- gate_weight: bfloat16 [128, 128], replicated, may hold values from -0.5 to 0.5
- out_gain: float32 [128], replicated, may hold values from 0.1 to 1.9
- out_weight: bfloat16 [128, 128], replicated, may hold values from -0.5 to 0.5
Outputs:
- mixed: bfloat16 [256, 2560, 128], P('row', 'col')
All inputs are finite; a program needn't handle non-finite values.
Results may differ from a plain program's by a relative error of at most 0.0078.
Values may be sent and summed in bfloat16 or wider, within the bound.
A program may use at most 192 MiB of HBM per device.

v0:
```python
import jax
import jax.numpy as jnp
from jax import lax
from jax.sharding import PartitionSpec as P

WIN_BLOCK = 8


def layer_norm(values, scales):
    floats = values.astype(jnp.float32)
    center = floats - jnp.mean(floats, axis=-1, keepdims=True)
    spread = jnp.mean(center * center, axis=-1, keepdims=True)
    return center * lax.rsqrt(spread + 1e-05) * scales


def gated_proj(inputs, weight):
    joined = jnp.einsum("rjc,ch->rjh", inputs, weight, preferred_element_type=jnp.float32)
    split_at = weight.shape[1] // 2
    return (jax.nn.sigmoid(joined[..., split_at:]) * joined[..., :split_at]).astype(jnp.bfloat16)


def shards(pair, in_gain, a_weight, b_weight, gate_weight, out_gain, out_weight):
    normed = layer_norm(pair, in_gain).astype(jnp.bfloat16)
    row_total, col_total, chan_total = normed.shape
    left_proj = gated_proj(normed[:, :WIN_BLOCK], a_weight)
    right_proj = gated_proj(normed, b_weight)
    block_count = row_total // col_total
    win_normed = normed.reshape(block_count, col_total, col_total, chan_total)[:, :WIN_BLOCK]
    win_normed = win_normed.reshape(block_count * WIN_BLOCK, col_total, chan_total)
    gate_vals = jax.nn.sigmoid(
        jnp.einsum("wjc,cd->wjd", win_normed, gate_weight, preferred_element_type=jnp.float32)
    )
    gathered = lax.all_gather(left_proj, "col", axis=1, tiled=True)
    summed = lax.psum_scatter(
        jnp.einsum("kwh,kjh->wjh", gathered, right_proj, preferred_element_type=jnp.float32),
        "row",
        scatter_dimension=0,
        tiled=True,
    )
    update_in = layer_norm(summed, out_gain).astype(jnp.bfloat16)
    projected = jnp.einsum("wjh,hc->wjc", update_in, out_weight, preferred_element_type=jnp.float32)
    return (gate_vals * projected).astype(jnp.bfloat16)


def solution(mesh):
    in_specs = (P("row", "col", None), P(), P(), P(), P(), P(), P())
    out_specs = P("row", "col", None)
    return jax.shard_map(shards, mesh=mesh, in_specs=in_specs, out_specs=out_specs, check_vma=False)
```

profile of v0, /device:TPU:160, one launch (start us, length us, event | category | flops | bytes accessed | tf_op | source)
XLA Modules:
  0.0 395.9 jit_solution(10127741851910120004)
XLA Ops:
  6.5 0.0 copy-start
  6.5 0.0 copy-start.7
  6.5 0.0 all-gather.2.cloned.1.call-start
  6.5 0.0 copy-start.2
  6.5 5.9 %convert_reduce_fusion = f32[320,80]{1,0:T(8,128)S(1)} fusion(bf16[320,80,128]{2,1,0:T(8,128)(2,1)} %param.7), kind=kLoop, calls=%fused_computation.1 | loop fusion | flops 6528000 | bytes 6656000 | tf_op jit(solution)/shard_map/reduce_sum | solution.py:11
  12.5 0.0 copy-done.2
  12.5 9.6 %fusion.2 = f32[320,80]{1,0:T(8,128)S(1)} fusion(bf16[320,80,128]{2,1,0:T(8,128)(2,1)S(1)} %copy-done.2, f32[320,80]{1,0:T(8,128)S(1)} %broadcast_multiply_fusion), kind=kLoop, calls=%fused_computation.4 | loop fusion | flops 13081600 | bytes 6758400 | tf_op jit(solution)/shard_map/reduce_sum | solution.py:12
  22.2 0.0 copy-done.7
  22.2 0.0 copy-start.4
  22.2 8.3 %fusion.4 = bf16[320,80,128]{2,1,0:T(8,128)(2,1)S(1)} fusion(bf16[320,80,128]{2,1,0:T(8,128)(2,1)S(1)} %copy-done.2, f32[128]{0:T(128)S(1)} %copy-done.7, f32[320,80]{1,0:T(8,128)S(1)} %add_rsqrt_fusion, f32[320,80]{1,0:T(8,128)S(1)} %broadcast_multiply_fusion), kind=kLoop, calls=%fused_computation.6 | loop fusion | flops 16384000 | bytes 13312512 | tf_op jit(solution)/shard_map/convert_element_type | solution.py:23
  30.5 0.0 copy-start.3
  30.5 2.7 copy-done.3
  33.2 0.0 copy-done.4
  33.2 0.5 fusion.17
  33.7 1.2 fusion.13
  34.9 0.0 all-gather.2.cloned.1.call-update
  34.9 0.2 reduce-scatter.2.cloned.1.call-start
  35.1 0.0 copy-done
  35.2 15.5 %fusion.23 = f32[320,80,256]{2,1,0:T(8,128)} fusion(bf16[320,80,128]{2,1,0:T(8,128)(2,1)} %copy-done.3, bf16[128,256]{1,0:T(8,128)(2,1)S(1)} %copy-done), kind=kOutput, calls=%fused_computation.36 | convolution fusion | flops 1677721600 | bytes 32833536 | tf_op jit(solution)/shard_map/rjc,ch->rjh/dot_general | solution.py:17
  50.6 13.0 %fusion.5 = bf16[320,80,128]{2,1,0:T(8,128)(2,1)} fusion(f32[320,80,256]{2,1,0:T(8,128)} %fusion.23), kind=kLoop, calls=%fused_computation.8 | loop fusion | flops 16384000 | bytes 32768000 | tf_op jit(solution)/shard_map/convert_element_type | solution.py:19
  63.7 11.7 %copy.11 = bf16[320,80,128]{0,1,2:T(8,128)(2,1)} copy(bf16[320,80,128]{2,1,0:T(8,128)(2,1)} %fusion.5) | data formatting | bytes 13107200 | tf_op jit(solution)/shard_map/convert_element_type | solution.py:19
  75.4 102.5 %all-gather.2.cloned.1.call-done = bf16[320,256,128]{2,1,0:T(8,128)(2,1)} async-done(((bf16[320,8,128]{2,1,0:T(8,128)(2,1)}), bf16[320,256,128]{2,1,0:T(8,128)(2,1)}) %all-gather.2.cloned.1.call-update) | async-done | bytes 20971536 | tf_op jit(solution)/shard_map/all_gather | solution.py:33
  177.9 34.5 %copy.12 = bf16[320,256,128]{0,1,2:T(8,128)(2,1)} copy(bf16[320,256,128]{2,1,0:T(8,128)(2,1)} %all-gather.2.cloned.1.call-done) | data formatting | bytes 41943040 | tf_op jit(solution)/shard_map/all_gather | solution.py:33
  212.4 18.2 %convolution_bitcast_fusion = f32[256,80,128]{0,1,2:T(8,128)} fusion(bf16[320,80,128]{0,1,2:T(8,128)(2,1)} %copy.11, bf16[320,256,128]{0,1,2:T(8,128)(2,1)} %copy.12), kind=kOutput, calls=%fused_computation.13 | convolution fusion | flops 1677721600 | bytes 38010880 | tf_op jit(solution)/shard_map/kwh,kjh->wjh/dot_general | solution.py:35
  230.6 12.2 %copy.13 = f32[256,80,128]{2,1,0:T(8,128)} copy(f32[256,80,128]{0,1,2:T(8,128)} %convolution_bitcast_fusion) | data formatting | bytes 20971520 | tf_op jit(solution)/shard_map/kwh,kjh->wjh/transpose | solution.py:35
  242.9 0.0 copy-start.8
  242.9 0.0 reduce-scatter.2.cloned.1.call-update
  242.9 0.0 copy-start.5
  242.9 0.0 copy-start.6
  242.9 0.0 copy-start.1
  242.9 1.2 slice.24
  244.1 0.0 copy-done.8
  244.1 0.5 fusion.11
  244.6 137.2 %reduce-scatter.2.cloned.1.call-done = f32[32,80,128]{2,1,0:T(8,128)} async-done(((f32[256,80,128]{2,1,0:T(8,128)}), f32[32,80,128]{2,1,0:T(8,128)}) %reduce-scatter.2.cloned.1.call-update) | async-done | bytes 1310736 | tf_op jit(solution)/shard_map/reduce_scatter | solution.py:34
  381.8 1.9 reduce_sum.38
  383.7 2.3 multiply_reduce_fusion
  386.0 0.0 copy-done.5
  386.1 0.0 copy-done.6
  386.1 3.0 fusion.12
  389.1 0.0 copy-done.1
  (4 shorter events, 0.1 us)
Async XLA Ops:
  6.5 28.6 %copy-start = (bf16[128,256]{1,0:T(8,128)(2,1)S(1)}, bf16[128,256]{1,0:T(8,128)(2,1)}, u32[]{:S(2)}) copy-start(bf16[128,256]{1,0:T(8,128)(2,1)} %param.10) | copy-start | bytes 196612
  6.5 15.6 %copy-start.7 = (f32[128]{0:T(128)S(1)}, f32[128]{0:T(128)}, u32[]{:S(2)}) copy-start(f32[128]{0:T(128)} %param.8) | copy-start | bytes 1540
  6.5 171.4 %all-gather.2.cloned.1.call-start = ((), (), s32[]{:S(2)}) async-start(), calls=%async_computation.1 | async-start | bytes 21626880 | tf_op jit(solution)/shard_map/all_gather | solution.py:33
  6.5 5.9 %copy-start.2 = (bf16[320,80,128]{2,1,0:T(8,128)(2,1)S(1)}, bf16[320,80,128]{2,1,0:T(8,128)(2,1)}, u32[]{:S(2)}) copy-start(bf16[320,80,128]{2,1,0:T(8,128)(2,1)} %param.7) | copy-start | bytes 19660804
  22.2 11.0 %copy-start.4 = (bf16[128,256]{1,0:T(8,128)(2,1)S(1)}, bf16[128,256]{1,0:T(8,128)(2,1)}, u32[]{:S(2)}) copy-start(bf16[128,256]{1,0:T(8,128)(2,1)} %param.9) | copy-start | bytes 196612
  30.5 2.7 copy-start.3
  34.9 346.9 %reduce-scatter.2.cloned.1.call-start = ((), (), s32[]{:S(2)}) async-start(), calls=%async_computation.2 | async-start | bytes 11796480 | tf_op jit(solution)/shard_map/reduce_scatter | solution.py:34
  242.9 1.2 copy-start.8
  242.9 143.2 %copy-start.5 = (bf16[128,128]{1,0:T(8,128)(2,1)S(1)}, bf16[128,128]{1,0:T(8,128)(2,1)}, u32[]{:S(2)}) copy-start(bf16[128,128]{1,0:T(8,128)(2,1)} %param.13) | copy-start | bytes 98308
  242.9 143.2 %copy-start.6 = (f32[128]{0:T(128)S(1)}, f32[128]{0:T(128)}, u32[]{:S(2)}) copy-start(f32[128]{0:T(128)} %param.12) | copy-start | bytes 1540
  242.9 146.2 %copy-start.1 = (bf16[128,256]{1,0:T(8,128)(2,1)S(1)}, bf16[128,256]{1,0:T(8,128)(2,1)}, u32[]{:S(2)}) copy-start(bf16[128,256]{1,0:T(8,128)(2,1)} %param.10) | copy-start | bytes 196612
Sparse Core Ops, SparseCore 0:
  35.0 142.8 all-gather.1
  243.0 138.7 reduce-scatter.1
where the time goes:
time: 399 us; the launch traced here: 396 us
  waiting for transfers between devices  240 us (60%)
  local copies, waits for them, and re-layouts  62.4 us (16%)
  other arithmetic  42.3 us (11%)
  matrix products  37.7 us (9%)
  between operations  13.6 us (3%)
    reduce_scatter x1, waiting for transfers between devices, shards(): lax.psum_scatter(jnp.einsum('kwh,kjh->wjh', gathered, right_proj, preferr...  137 us
    all_gather x1, waiting for transfers between devices, shards(): gathered = lax.all_gather(left_proj, 'col', axis=1, tiled=True)  102 us
    all_gather x1, local copies, waits for them, and re-layouts, shards(): gathered = lax.all_gather(left_proj, 'col', axis=1, tiled=True)  34.5 us
    dot_general x1, matrix products, shards(): jnp.einsum('kwh,kjh->wjh', gathered, right_proj, preferred_element_type=j...  18.2 us
    dot_general x2, matrix products, gated_proj(): jnp.einsum('rjc,ch->rjh', inputs, weight, preferred_element_type=jnp.floa...  16 us
    convert_element_type x2, other arithmetic, gated_proj(): (jax.nn.sigmoid(joined[..., split_at:]) * joined[..., :split_at]).astype(...  14.2 us
    transpose x1, local copies, waits for them, and re-layouts, shards(): jnp.einsum('kwh,kjh->wjh', gathered, right_proj, preferred_element_type=j...  12.2 us
    reduce_sum x2, other arithmetic, layer_norm(): spread = jnp.mean(center * center, axis=-1, keepdims=True)  11.9 us
  transfers between devices with their start and end apart: 2, of which 2 were waited for; matrix products, arithmetic and copies ran while one was open for 11% of the time, Pallas kernels for 0%

commit v1 on v0

v1 whole, which is shorter than its diff:
```python
import functools

import jax
import jax.numpy as jnp
from jax import lax
from jax.experimental import pallas as pl
from jax.experimental.pallas import tpu as pltpu
from jax.sharding import PartitionSpec as P

MESH = pl.DeviceIdType.MESH
BF = jnp.bfloat16
F32 = jnp.float32
EPS = 1e-05
KB = 16


def sigmoid(v):
    return 0.5 * jnp.tanh(0.5 * v) + 0.5


def norm_lanes(v, gain):
    f = v.astype(F32)
    f = f - jnp.mean(f, axis=-1, keepdims=True)
    spread = jnp.mean(f * f, axis=-1, keepdims=True)
    return f * lax.rsqrt(spread + EPS) * gain


def dot_nt(a, b):
    return lax.dot_general(a, b, (((1,), (1,)), ((), ())), preferred_element_type=F32)


def kernel(pair, in_gain, a_w, b_w, g_w, out_gain, o_w, out,
           win, pbuf, gwin, wat, wbt, t1, t2, tr, lbuf, rbuf, sbuf, ybuf, xhs, xhr, fbuf, ubuf, gates,
           win_sem, p_sem, g_sem, zs, zr, xs_, xr, cs, cr, ys, yr, hs, hr):
    row = lax.axis_index("row")
    col = lax.axis_index("col")
    y, xh = row // 2, row % 2
    x, z, c = col // 16, (col // 2) % 8, col % 2

    def dev(y_, xh_, x_, z_, c_):
        return (y_ * 2 + xh_, (x_ * 8 + z_) * 2 + c_)

    up = dev(y, xh, x, (z + 1) % 8, c)
    down = dev(y, xh, x, (z + 7) % 8, c)
    across = dev(y, xh, 1 - x, z, c)
    mate = dev(y, xh, x, z, 1 - c)
    twin = dev(y, 1 - xh, x, z, c)
    others = [dev((y + d) % 4, xh, x, z, c) for d in (1, 2, 3)]

    win_copy = pltpu.make_async_copy(pair.at[:, 0:16, :], win, win_sem)
    win_copy.start()

    def p_copy(step):
        slot = step % 2
        return pltpu.make_async_copy(pair.at[pl.ds(step * KB, KB)], pbuf.at[slot], p_sem.at[slot])

    p_copy(0).start()
    g_copies = [pltpu.make_async_copy(pair.at[80 * b:80 * b + 8], gwin.at[b], g_sem.at[b]) for b in range(4)]
    for copy in g_copies:
        copy.start()

    barrier = pltpu.get_barrier_semaphore()
    for d in [up, down, across, mate, twin] + others:
        pl.semaphore_signal(barrier, inc=1, device_id=d, device_id_type=MESH)

    lane = lax.broadcasted_iota(jnp.int32, (8, 128), 1)
    lane16 = lax.broadcasted_iota(jnp.int32, (16, 128), 1)
    gain = in_gain[...]

    wat[...] = a_w[...].astype(F32).T.astype(BF)
    t2[0:256, :] = b_w[...].astype(F32).T
    wbt[0:128, :] = t2[pl.ds(0, 128, stride=2), :].astype(BF)
    wbt[128:256, :] = t2[pl.ds(1, 128, stride=2), :].astype(BF)

    win_copy.wait()

    @pl.loop(0, 10)
    def _(i):
        v = win[pl.ds(i * 32, 32)].astype(F32)[:, 0:8, :]
        t1[pl.ds(pl.multiple_of(i * 256, 256), 256), :] = norm_lanes(v, gain).reshape(256, 128)

    t1[2560:3072, :] = jnp.zeros((512, 128), F32)
    for w in range(8):
        xw = t1[pl.ds(w, 384, stride=8), :].astype(BF)
        v = dot_nt(wat[...], xw)
        v = sigmoid(v[128:]) * v[:128]
        for t in range(3):
            t2[pl.ds(1024 * t + w, 128, stride=8), :] = v[:, t * 128:(t + 1) * 128]

    def slot(x_, z_, c_):
        return (x_ * 8 + z_) * 2 + c_

    mine = slot(x, z, c)

    @pl.loop(0, 32)
    def _(q):
        base = pl.multiple_of(q * 32, 32)
        lbuf[mine, q, 0:32, :] = t2[pl.ds(base, 32), :].astype(BF)
        lbuf[mine, q, 32:64, :] = t2[pl.ds(1024 + base, 32), :].astype(BF)
        low = t2[pl.ds(2048 + base, 16), :]
        high = pltpu.roll(t2[pl.ds(2048 + base + 16, 16), :], 64, 1)
        lbuf[mine, q, 64:80, :] = jnp.where(lane16 < 64, low, high).astype(BF)

    pl.semaphore_wait(barrier, 8)

    A, B = (0, 16), (16, 16)
    CU, CD = (0, 8), (8, 8)

    def part(x_, z_, c_, piece):
        return lbuf.at[slot(x_, z_, c_), pl.ds(piece[0], piece[1])]

    def z_copy(direction, n, k):
        origin = (z + 8 - n) % 8 if direction == 0 else (z + n) % 8
        if k == 2:
            piece = A if n < 3 else (CU if direction == 0 else CD)
            ref = part(1 - x, origin, c, piece)
        else:
            ref = part(x, origin, c, (A, B)[k])
        return pltpu.make_async_remote_copy(
            src_ref=ref, dst_ref=ref, send_sem=zs.at[direction, n, k], recv_sem=zr.at[direction, n, k],
            device_id=up if direction == 0 else down, device_id_type=MESH)

    def z_arrival(direction, n, k):
        origin = (z + 8 - (n + 1)) % 8 if direction == 0 else (z + n + 1) % 8
        if k == 2:
            piece = A if n < 3 else (CU if direction == 0 else CD)
            ref = part(1 - x, origin, c, piece)
        else:
            ref = part(x, origin, c, (A, B)[k])
        return pltpu.make_async_remote_copy(
            src_ref=ref, dst_ref=ref, send_sem=zs.at[direction, n, k], recv_sem=zr.at[direction, n, k],
            device_id=up if direction == 0 else down, device_id_type=MESH)

    def at(o):
        return (z + o) % 8

    def x_copy(o, piece, k):
        ref = part(x, at(o), c, piece)
        return pltpu.make_async_remote_copy(
            src_ref=ref, dst_ref=ref, send_sem=xs_.at[k], recv_sem=xr.at[k], device_id=across, device_id_type=MESH)

    def x_arrival(o, piece, k):
        ref = part(1 - x, at(o), c, piece)
        return pltpu.make_async_remote_copy(
            src_ref=ref, dst_ref=ref, send_sem=xs_.at[k], recv_sem=xr.at[k], device_id=across, device_id_type=MESH)

    def c_copy(side, o, piece, k):
        ref = part(x if side == 0 else 1 - x, at(o), c, piece)
        return pltpu.make_async_remote_copy(
            src_ref=ref, dst_ref=ref, send_sem=cs.at[side, o, k], recv_sem=cr.at[side, o, k],
            device_id=mate, device_id_type=MESH)

    def c_arrival(side, o, piece, k):
        ref = part(x if side == 0 else 1 - x, at(o), 1 - c, piece)
        return pltpu.make_async_remote_copy(
            src_ref=ref, dst_ref=ref, send_sem=cs.at[side, o, k], recv_sem=cr.at[side, o, k],
            device_id=mate, device_id_type=MESH)

    sent = []

    def go(copy):
        copy.start()
        sent.append(copy)

    def c_pieces(side, o):
        if side == 1 and o == 4:
            return [(CU, 0), (CD, 2), (B, 1)]
        return [(A, 0), (B, 1)]

    def serve(n, k):
        for direction in (0, 1):
            if n == 3 and k == (1 if direction == 0 else 0):
                continue
            z_arrival(direction, n, k).wait_recv()
            if n < 2 or (n == 2 and not k == (1 if direction == 0 else 0)):
                go(z_copy(direction, n + 1, k))
            o = (8 - (n + 1)) % 8 if direction == 0 else n + 1
            if k == 0:
                go(c_copy(0, o, A, 0))
            elif k == 1:
                go(x_copy(o, B, o))
                go(c_copy(0, o, B, 1))
            elif n < 3:
                go(c_copy(1, o, A, 0))
            else:
                go(c_copy(1, o, CU if direction == 0 else CD, 0 if direction == 0 else 2))

    def serve_x(o):
        x_arrival(o, B, o).wait_recv()
        go(c_copy(1, o, B, 1))

    def have(o):
        for side in (0, 1):
            for piece, k in c_pieces(side, o):
                c_arrival(side, o, piece, k).wait_recv()

    go(x_copy(0, A, 8))
    for direction in (0, 1):
        go(z_copy(direction, 0, 0))
    for direction in (0, 1):
        go(z_copy(direction, 0, 1))
    go(x_copy(0, B, 0))
    go(c_copy(0, 0, A, 0))
    go(c_copy(0, 0, B, 1))

    rbuf[:, 0, 320:384, :] = jnp.zeros((32, 64, 256), BF)
    rbuf[:, 1, 256:320, :] = jnp.zeros((32, 64, 256), BF)

    def right_step(step, tail):
        @pl.when(step + 1 < 20)
        def _():
            p_copy(step + 1).start()

        p_copy(step).wait()
        here = step % 2
        for pairs in range(KB // 2):
            first, second = [], []
            for kk in (2 * pairs, 2 * pairs + 1):
                v = norm_lanes(pbuf[here, kk], gain).astype(BF)
                main, rest = v[0:64], v[64:80]
                first += [main, rest, rest, rest, rest]
                second += [rest, rest, rest, rest, main]
            for par, rows in ((0, first), (1, second)):
                v = dot_nt(wbt[par * 128:(par + 1) * 128, :], jnp.concatenate(rows, axis=0))
                v = sigmoid(v[64:]) * v[:64]
                for half in (0, 1):
                    tr[pl.ds(par * 1024 + 2 * pairs + half, 64, stride=KB), :] = v[:, half * 128:(half + 1) * 128]
        for par in (0, 1):
            v = tr[par * 1024:(par + 1) * 1024, :].astype(BF).reshape(32, 2, KB, 128)
            base = pl.multiple_of(step * KB, KB)
            for i in (0, 1):
                where = base + 64 if (tail and i == 1) else base
                rbuf[:, i, pl.ds(pl.multiple_of(where, KB), KB), par * 128:(par + 1) * 128] = v[:, i]

    def right_steps(lo, hi, tail=False):
        @pl.loop(lo, hi)
        def _(step):
            right_step(step, tail)

    right_steps(0, 5)
    x_arrival(0, A, 8).wait_recv()
    for direction in (0, 1):
        go(z_copy(direction, 0, 2))
    go(c_copy(1, 0, A, 0))
    right_steps(5, 9)
    serve(0, 0)
    right_steps(9, 13)
    serve_x(0)
    serve(0, 1)
    right_steps(13, 16)
    right_steps(16, 20, True)
    serve(0, 2)
    serve_x(1)
    serve_x(7)

    for copy in g_copies:
        copy.wait()

    @pl.loop(0, 32)
    def _(i):
        v = norm_lanes(gwin[i // 8, i % 8], gain).astype(BF)
        gates[i] = sigmoid(jnp.dot(v, g_w[...], preferred_element_type=F32))

    def contract(chips):
        @pl.loop(0, 16)
        def _(o):
            tails = [[None, None] for _ in chips]
            for m in range(4):
                q, i = o * 2 + m // 2, m % 2
                lhs = []
                for lane_tile in range(3):
                    start = 64 if lane_tile == 2 else 32 * lane_tile + 16 * i
                    lhs.append(jnp.concatenate(
                        [lbuf[slot(cx, cz, cc), q, start:start + 16, :] for cx, cz in chips for cc in (0, 1)], axis=0))
                res = jnp.dot(jnp.concatenate(lhs, axis=1), rbuf[q, i], preferred_element_type=F32)
                for ci, (cx, cz) in enumerate(chips):
                    both = []
                    for cc in (0, 1):
                        base = (ci * 2 + cc) * 16
                        even = res[base:base + 8, 0:128]
                        odd = res[base + 8:base + 16, 128:256]
                        both.append(jnp.where(lane < 64, even, odd))
                        mix = jnp.where(lane < 64, odd, even)
                        old = tails[ci][cc]
                        tails[ci][cc] = mix if old is None else jnp.where((lane % 64) // 16 == m, mix, old)
                    sbuf[cx * 8 + cz, o, 16 * m:16 * m + 16, :] = jnp.concatenate(both, axis=0).astype(BF)
            for ci, (cx, cz) in enumerate(chips):
                sbuf[cx * 8 + cz, o, 64:80, :] = jnp.concatenate(tails[ci], axis=0).astype(BF)

    def y_copy(cx, cz):
        target = cx * 2 + cz // 4
        rel = (y + 4 - target) % 4
        return target, pltpu.make_async_remote_copy(
            src_ref=sbuf.at[cx * 8 + cz], dst_ref=ybuf.at[rel, cz % 4],
            send_sem=ys.at[cx * 8 + cz], recv_sem=yr.at[rel, cz % 4],
            device_id=dev(target, xh, x, z, c), device_id_type=MESH)

    def send_sums(cx, cz):
        target, copy = y_copy(cx, cz)

        @pl.when(target != y)
        def _():
            copy.start()

    def group(offsets):
        chips = [(cx, at(o)) for o in offsets for cx in (0, 1)]
        contract(chips)
        for cx, cz in chips:
            send_sums(cx, cz)

    have(0)
    group([0])
    serve(1, 0)
    serve(1, 1)
    have(1)
    have(7)
    group([1, 7])
    serve(1, 2)
    serve_x(2)
    serve_x(6)
    serve(2, 0)
    have(2)
    have(6)
    group([2, 6])
    serve(2, 1)
    serve(2, 2)
    serve_x(3)
    serve_x(5)
    have(3)
    have(5)
    group([3, 5])
    serve(3, 0)
    serve(3, 1)
    serve(3, 2)
    serve_x(4)
    have(4)
    group([4])

    def total(zi, o):
        v = sbuf[(y // 2) * 8 + (y % 2) * 4 + zi, o].astype(F32)
        for rel in (1, 2, 3):
            v += ybuf[rel, zi, o].astype(F32)
        return v

    def y_wait(zi):
        for rel in (1, 2, 3):
            pltpu.make_async_remote_copy(
                src_ref=ybuf.at[rel, zi], dst_ref=ybuf.at[rel, zi], send_sem=ys.at[0], recv_sem=yr.at[rel, zi],
                device_id=twin, device_id_type=MESH).wait_recv()

    def h_copy(zz):
        return pltpu.make_async_remote_copy(
            src_ref=xhs.at[zz], dst_ref=xhr.at[zz], send_sem=hs.at[zz], recv_sem=hr.at[zz],
            device_id=twin, device_id_type=MESH)

    for zz in (0, 1):
        zi = (1 - xh) * 2 + zz
        y_wait(zi)

        @pl.loop(0, 16)
        def _(o):
            xhs[zz, o] = total(zi, o).astype(BF)

        go(h_copy(zz))

    for zz in (0, 1):
        zi = xh * 2 + zz
        y_wait(zi)

        @pl.loop(0, 16)
        def _(o):
            fbuf[zz, o] = total(zi, o)

    gain_col = jnp.broadcast_to(out_gain[...], (128, 128)).T

    for zz in (0, 1):
        h_copy(zz).wait_recv()

        @pl.loop(0, 16)
        def _(o):
            v = fbuf[zz, o] + xhr[zz, o].astype(F32)
            rest = v[64:80]
            for m in range(4):
                main = v[16 * m:16 * m + 16]
                even = jnp.where(lane16 < 64, main, pltpu.roll(rest, (128 - 16 * m) % 128, 1))
                odd = jnp.where(lane16 < 64, pltpu.roll(main, 64, 1), pltpu.roll(rest, 64 - 16 * m, 1))
                base = (o * 8 + 2 * m) * 16
                ubuf[pl.ds(pl.multiple_of(base, 16), 16), :] = even
                ubuf[pl.ds(pl.multiple_of(base + 16, 16), 16), :] = odd

        @pl.loop(0, 16)
        def _(r):
            u = ubuf[pl.ds(r, 128, stride=16), :]
            u = u - jnp.mean(u, axis=0, keepdims=True)
            spread = jnp.mean(u * u, axis=0, keepdims=True)
            u = (u * lax.rsqrt(spread + EPS) * gain_col).T[0:80].astype(BF)
            v = jnp.dot(u, o_w[...], preferred_element_type=F32)
            out[zz * 16 + r] = (gates[zz * 16 + r] * v).astype(BF)

    for copy in sent:
        copy.wait_send()
    for cx in (0, 1):
        for o in range(8):
            target, copy = y_copy(cx, at(o))

            @pl.when(target != y)
            def _():
                copy.wait_send()


def step(pair, in_gain, a_w, b_w, g_w, out_gain, o_w):
    vmem = pl.BlockSpec(memory_space=pltpu.VMEM)
    dma = pltpu.SemaphoreType.DMA
    return pl.pallas_call(
        kernel,
        out_shape=jax.ShapeDtypeStruct((32, 80, 128), BF),
        in_specs=[pl.BlockSpec(memory_space=pl.ANY)] + [vmem] * 6,
        out_specs=vmem,
        scratch_shapes=[
            pltpu.VMEM((320, 16, 128), BF),
            pltpu.VMEM((2, KB, 80, 128), BF),
            pltpu.VMEM((4, 8, 80, 128), BF),
            pltpu.VMEM((256, 128), BF),
            pltpu.VMEM((256, 128), BF),
            pltpu.VMEM((3072, 128), F32),
            pltpu.VMEM((3072, 128), F32),
            pltpu.VMEM((2048, 128), F32),
            pltpu.VMEM((32, 32, 80, 128), BF),
            pltpu.VMEM((32, 2, 384, 256), BF),
            pltpu.VMEM((16, 16, 80, 128), BF),
            pltpu.VMEM((4, 4, 16, 80, 128), BF),
            pltpu.VMEM((2, 16, 80, 128), BF),
            pltpu.VMEM((2, 16, 80, 128), BF),
            pltpu.VMEM((2, 16, 80, 128), F32),
            pltpu.VMEM((2048, 128), F32),
            pltpu.VMEM((32, 80, 128), F32),
            dma, dma((2,)), dma((4,)),
            dma((2, 4, 3)), dma((2, 4, 3)),
            dma((9,)), dma((9,)),
            dma((2, 8, 3)), dma((2, 8, 3)),
            dma((16,)), dma((4, 4)),
            dma((2,)), dma((2,)),
        ],
        compiler_params=pltpu.CompilerParams(
            collective_id=0, has_side_effects=True, vmem_limit_bytes=63 * 2 ** 20),
        name="triangle",
    )(pair, in_gain.reshape(1, 128), a_w, b_w, g_w, out_gain.reshape(1, 128), o_w)


def solution(mesh):
    in_specs = (P("row", "col", None), P(), P(), P(), P(), P(), P())
    return jax.shard_map(step, mesh=mesh, in_specs=in_specs, out_specs=P("row", "col", None), check_vma=False)
```

time: 399 us -> 169 us (0.42)
  the two profiles are of different devices: /device:TPU:160 before, /device:TPU:198 now
where the time goes in v1:
time: 169 us
  Pallas kernels  167 us (99%)
  local copies, waits for them, and re-layouts  1.97 us (1%)
    pallas_call x1, Pallas kernels, step(): pl.pallas_call(kernel, out_shape=jax.ShapeDtypeStruct((32, 80, 128), BF),...  167 us

profile of v1, /device:TPU:198, one launch (start us, length us, event | category | flops | bytes accessed | tf_op | source)
XLA Modules:
  0.0 169.1 jit_solution(8112223458693502066)
XLA Ops:
  0.0 167.1 %triangle.1 = bf16[32,80,128]{2,1,0:T(8,128)(2,1)} custom-call(bf16[320,80,128]{2,1,0:T(8,128)(2,1)} %pair.1, f32[1,128]{1,0:T(1,128)} %bitcast.2, bf16[128,256]{1,0:T(8,128)(2,1)} %a_w.1, bf16[128,256]{1,0:T(8,128)(2,1)} %b_w.1, bf16[128,128]{1,0:T(8,128)(2,1)} %g_w.1, f32[1,128]{1,0:T(1,128)} %bitcast.3, bf16[128,128]{1,0:T(8,128)(2,1)} %o_w.1), custom_call_target="tpu_custom_call" | custom-call | tf_op jit(solution)/shard_map/triangle/pallas_call | solution.py:414
  167.1 2.0 %copy.9 = bf16[32,80,128]{2,1,0:T(8,128)(2,1)} copy(bf16[32,80,128]{2,1,0:T(8,128)(2,1)} %triangle.1) | data formatting | bytes 1310720

commit v2 on v1

--- a/solution.py
+++ b/solution.py
@@ -189,10 +189,11 @@
         x_arrival(o, B, o).wait_recv()
         go(c_copy(1, o, B, 1))
 
-    def have(o):
+    def have(o, half):
         for side in (0, 1):
             for piece, k in c_pieces(side, o):
-                c_arrival(side, o, piece, k).wait_recv()
+                if (k == 1) == (half == 1):
+                    c_arrival(side, o, piece, k).wait_recv()
 
     go(x_copy(0, A, 8))
     for direction in (0, 1):
@@ -237,32 +238,22 @@
         def _(step):
             right_step(step, tail)
 
-    right_steps(0, 5)
+    right_steps(0, 4)
     x_arrival(0, A, 8).wait_recv()
     for direction in (0, 1):
         go(z_copy(direction, 0, 2))
     go(c_copy(1, 0, A, 0))
-    right_steps(5, 9)
+    right_steps(4, 8)
     serve(0, 0)
-    right_steps(9, 13)
+    right_steps(8, 12)
     serve_x(0)
+    right_steps(12, 16)
+    serve(0, 2)
     serve(0, 1)
-    right_steps(13, 16)
     right_steps(16, 20, True)
-    serve(0, 2)
-    serve_x(1)
-    serve_x(7)
-
-    for copy in g_copies:
-        copy.wait()
-
-    @pl.loop(0, 32)
-    def _(i):
-        v = norm_lanes(gwin[i // 8, i % 8], gain).astype(BF)
-        gates[i] = sigmoid(jnp.dot(v, g_w[...], preferred_element_type=F32))
-
-    def contract(chips):
-        @pl.loop(0, 16)
+
+    def contract(chips, half):
+        @pl.loop(8 * half, 8 * half + 8)
         def _(o):
             tails = [[None, None] for _ in chips]
             for m in range(4):
@@ -287,54 +278,29 @@
             for ci, (cx, cz) in enumerate(chips):
                 sbuf[cx * 8 + cz, o, 64:80, :] = jnp.concatenate(tails[ci], axis=0).astype(BF)
 
-    def y_copy(cx, cz):
+    def y_copy(cx, cz, half):
         target = cx * 2 + cz // 4
         rel = (y + 4 - target) % 4
+        octets = pl.ds(8 * half, 8)
         return target, pltpu.make_async_remote_copy(
-            src_ref=sbuf.at[cx * 8 + cz], dst_ref=ybuf.at[rel, cz % 4],
-            send_sem=ys.at[cx * 8 + cz], recv_sem=yr.at[rel, cz % 4],
+            src_ref=sbuf.at[cx * 8 + cz, octets], dst_ref=ybuf.at[rel, cz % 4, octets],
+            send_sem=ys.at[cx * 8 + cz, half], recv_sem=yr.at[rel, cz % 4, half],
             device_id=dev(target, xh, x, z, c), device_id_type=MESH)
 
-    def send_sums(cx, cz):
-        target, copy = y_copy(cx, cz)
+    def send_sums(cx, cz, half):
+        target, copy = y_copy(cx, cz, half)
 
         @pl.when(target != y)
         def _():
             copy.start()
 
-    def group(offsets):
+    def group(offsets, half):
+        for o in offsets:
+            have(o, half)
         chips = [(cx, at(o)) for o in offsets for cx in (0, 1)]
-        contract(chips)
+        contract(chips, half)
         for cx, cz in chips:
-            send_sums(cx, cz)
-
-    have(0)
-    group([0])
-    serve(1, 0)
-    serve(1, 1)
-    have(1)
-    have(7)
-    group([1, 7])
-    serve(1, 2)
-    serve_x(2)
-    serve_x(6)
-    serve(2, 0)
-    have(2)
-    have(6)
-    group([2, 6])
-    serve(2, 1)
-    serve(2, 2)
-    serve_x(3)
-    serve_x(5)
-    have(3)
-    have(5)
-    group([3, 5])
-    serve(3, 0)
-    serve(3, 1)
-    serve(3, 2)
-    serve_x(4)
-    have(4)
-    group([4])
+            send_sums(cx, cz, half)
 
     def total(zi, o):
         v = sbuf[(y // 2) * 8 + (y % 2) * 4 + zi, o].astype(F32)
@@ -342,41 +308,55 @@
             v += ybuf[rel, zi, o].astype(F32)
         return v
 
-    def y_wait(zi):
-        for rel in (1, 2, 3):
-            pltpu.make_async_remote_copy(
-                src_ref=ybuf.at[rel, zi], dst_ref=ybuf.at[rel, zi], send_sem=ys.at[0], recv_sem=yr.at[rel, zi],
-                device_id=twin, device_id_type=MESH).wait_recv()
-
-    def h_copy(zz):
-        return pltpu.make_async_remote_copy(
-            src_ref=xhs.at[zz], dst_ref=xhr.at[zz], send_sem=hs.at[zz], recv_sem=hr.at[zz],
-            device_id=twin, device_id_type=MESH)
-
-    for zz in (0, 1):
-        zi = (1 - xh) * 2 + zz
-        y_wait(zi)
-
-        @pl.loop(0, 16)
-        def _(o):
-            xhs[zz, o] = total(zi, o).astype(BF)
-
-        go(h_copy(zz))
-
-    for zz in (0, 1):
-        zi = xh * 2 + zz
-        y_wait(zi)
-
-        @pl.loop(0, 16)
-        def _(o):
-            fbuf[zz, o] = total(zi, o)
-
-    gain_col = jnp.broadcast_to(out_gain[...], (128, 128)).T
-
-    for zz in (0, 1):
-        h_copy(zz).wait_recv()
-
-        @pl.loop(0, 16)
+    def h_copy(zz, half):
+        octets = pl.ds(8 * half, 8)
+        return pltpu.make_async_remote_copy(
+            src_ref=xhs.at[zz, octets], dst_ref=xhr.at[zz, octets], send_sem=hs.at[zz, half],
+            recv_sem=hr.at[zz, half], device_id=twin, device_id_type=MESH)
+
+    def collect(offsets, half):
+        for off in offsets:
+            cz = at(off)
+            zi = cz % 4
+            zz = zi % 2
+
+            @pl.when(cz // 4 == y % 2)
+            def _():
+                for rel in (1, 2, 3):
+                    octets = pl.ds(8 * half, 8)
+                    pltpu.make_async_remote_copy(
+                        src_ref=ybuf.at[rel, zi, octets], dst_ref=ybuf.at[rel, zi, octets],
+                        send_sem=ys.at[0, half], recv_sem=yr.at[rel, zi, half],
+                        device_id=twin, device_id_type=MESH).wait_recv()
+
+                @pl.when(zi // 2 == xh)
+                def _():
+                    @pl.loop(8 * half, 8 * half + 8, unroll=2)
+                    def _(o):
+                        fbuf[zz, o] = total(zi, o)
+
+                @pl.when(zi // 2 != xh)
+                def _():
+                    @pl.loop(8 * half, 8 * half + 8, unroll=2)
+                    def _(o):
+                        xhs[zz, o] = total(zi, o).astype(BF)
+
+                    h_copy(zz, half).start()
+
+    def make_gates():
+        for copy in g_copies:
+            copy.wait()
+
+        @pl.loop(0, 32, unroll=4)
+        def _(i):
+            v = norm_lanes(gwin[i // 8, i % 8], gain).astype(BF)
+            gates[i] = sigmoid(jnp.dot(v, g_w[...], preferred_element_type=F32))
+
+    def finish(zz):
+        for half in (0, 1):
+            h_copy(zz, half).wait_recv()
+
+        @pl.loop(0, 16, unroll=2)
         def _(o):
             v = fbuf[zz, o] + xhr[zz, o].astype(F32)
             rest = v[64:80]
@@ -388,7 +368,7 @@
                 ubuf[pl.ds(pl.multiple_of(base, 16), 16), :] = even
                 ubuf[pl.ds(pl.multiple_of(base + 16, 16), 16), :] = odd
 
-        @pl.loop(0, 16)
+        @pl.loop(0, 16, unroll=4)
         def _(r):
             u = ubuf[pl.ds(r, 128, stride=16), :]
             u = u - jnp.mean(u, axis=0, keepdims=True)
@@ -397,15 +377,63 @@
             v = jnp.dot(u, o_w[...], preferred_element_type=F32)
             out[zz * 16 + r] = (gates[zz * 16 + r] * v).astype(BF)
 
+    gain_col = jnp.broadcast_to(out_gain[...], (128, 128)).T
+
+    group([0], 0)
+    group([0], 1)
+    serve(1, 0)
+    group([1, 7], 0)
+    collect([0], 0)
+    serve_x(1)
+    serve_x(7)
+    serve(1, 2)
+    group([1, 7], 1)
+    collect([0], 1)
+    serve(1, 1)
+    make_gates()
+    serve(2, 0)
+    group([2, 6], 0)
+    collect([1, 7], 0)
+    serve_x(2)
+    serve_x(6)
+    serve(2, 2)
+    group([2, 6], 1)
+    collect([1, 7], 1)
+    serve(2, 1)
+    serve(3, 0)
+    group([3, 5], 0)
+    serve_x(3)
+    serve_x(5)
+    serve(3, 1)
+    group([3, 5], 1)
+    collect([2, 6], 0)
+    serve(3, 2)
+    group([4], 0)
+    serve_x(4)
+    group([4], 1)
+    collect([2, 6], 1)
+    collect([3, 5], 0)
+    collect([3, 5], 1)
+
+    place = (z + 8 - ((y % 2) * 4 + xh * 2)) % 8
+    far = jnp.where((place >= 1) & (place <= 4), 0, 1)
+    finish(1 - far)
+    collect([4], 0)
+    collect([4], 1)
+    finish(far)
+
     for copy in sent:
         copy.wait_send()
-    for cx in (0, 1):
-        for o in range(8):
-            target, copy = y_copy(cx, at(o))
-
-            @pl.when(target != y)
-            def _():
-                copy.wait_send()
+    for half in (0, 1):
+        for zz in (0, 1):
+            h_copy(zz, half).wait_send()
+        for cx in (0, 1):
+            for o in range(8):
+                target, copy = y_copy(cx, at(o), half)
+
+                @pl.when(target != y)
+                def _():
+                    copy.wait_send()
 
 
 def step(pair, in_gain, a_w, b_w, g_w, out_gain, o_w):
@@ -438,8 +466,8 @@
             dma((2, 4, 3)), dma((2, 4, 3)),
             dma((9,)), dma((9,)),
             dma((2, 8, 3)), dma((2, 8, 3)),
-            dma((16,)), dma((4, 4)),
-            dma((2,)), dma((2,)),
+            dma((16, 2)), dma((4, 4, 2)),
+            dma((2, 2)), dma((2, 2)),
         ],
         compiler_params=pltpu.CompilerParams(
             collective_id=0, has_side_effects=True, vmem_limit_bytes=63 * 2 ** 20),

time: 169 us -> 146 us (0.86)
  the two profiles are of different devices: /device:TPU:198 before, /device:TPU:160 now
where the time goes in v2:
time: 146 us
  Pallas kernels  144 us (99%)
  local copies, waits for them, and re-layouts  1.97 us (1%)
    pallas_call x1, Pallas kernels, step(): pl.pallas_call(kernel, out_shape=jax.ShapeDtypeStruct((32, 80, 128), BF),...  144 us

profile of v2, /device:TPU:160, one launch (start us, length us, event | category | flops | bytes accessed | tf_op | source)
XLA Modules:
  0.0 146.1 jit_solution(2834679291152230193)
XLA Ops:
  0.0 144.1 %triangle.1 = bf16[32,80,128]{2,1,0:T(8,128)(2,1)} custom-call(bf16[320,80,128]{2,1,0:T(8,128)(2,1)} %pair.1, f32[1,128]{1,0:T(1,128)} %bitcast.2, bf16[128,256]{1,0:T(8,128)(2,1)} %a_w.1, bf16[128,256]{1,0:T(8,128)(2,1)} %b_w.1, bf16[128,128]{1,0:T(8,128)(2,1)} %g_w.1, f32[1,128]{1,0:T(1,128)} %bitcast.3, bf16[128,128]{1,0:T(8,128)(2,1)} %o_w.1), custom_call_target="tpu_custom_call" | custom-call | tf_op jit(solution)/shard_map/triangle/pallas_call | solution.py:442
  144.1 2.0 %copy.9 = bf16[32,80,128]{2,1,0:T(8,128)(2,1)} copy(bf16[32,80,128]{2,1,0:T(8,128)(2,1)} %triangle.1) | data formatting | bytes 1310720

commit v3 on v2

--- a/solution.py
+++ b/solution.py
@@ -74,59 +74,57 @@
 
     win_copy.wait()
 
-    @pl.loop(0, 10)
+    @pl.loop(0, 10, unroll=2)
     def _(i):
         v = win[pl.ds(i * 32, 32)].astype(F32)[:, 0:8, :]
         t1[pl.ds(pl.multiple_of(i * 256, 256), 256), :] = norm_lanes(v, gain).reshape(256, 128)
 
     t1[2560:3072, :] = jnp.zeros((512, 128), F32)
-    for w in range(8):
-        xw = t1[pl.ds(w, 384, stride=8), :].astype(BF)
-        v = dot_nt(wat[...], xw)
-        v = sigmoid(v[128:]) * v[:128]
-        for t in range(3):
-            t2[pl.ds(1024 * t + w, 128, stride=8), :] = v[:, t * 128:(t + 1) * 128]
-
     def slot(x_, z_, c_):
         return (x_ * 8 + z_) * 2 + c_
 
     mine = slot(x, z, c)
 
-    @pl.loop(0, 32)
-    def _(q):
-        base = pl.multiple_of(q * 32, 32)
-        lbuf[mine, q, 0:32, :] = t2[pl.ds(base, 32), :].astype(BF)
-        lbuf[mine, q, 32:64, :] = t2[pl.ds(1024 + base, 32), :].astype(BF)
-        low = t2[pl.ds(2048 + base, 16), :]
-        high = pltpu.roll(t2[pl.ds(2048 + base + 16, 16), :], 64, 1)
-        lbuf[mine, q, 64:80, :] = jnp.where(lane16 < 64, low, high).astype(BF)
-
-    pl.semaphore_wait(barrier, 8)
+    def left_half(half):
+        h0 = half * 64
+        weights = jnp.concatenate([wat[h0:h0 + 64, :], wat[128 + h0:192 + h0, :]], axis=0)
+        for w in range(8):
+            xw = t1[pl.ds(w, 384, stride=8), :].astype(BF)
+            v = dot_nt(weights, xw)
+            v = sigmoid(v[64:]) * v[:64]
+            for t in range(3):
+                t2[pl.ds(1024 * t + 8 * h0 + w, 64, stride=8), :] = v[:, t * 128:(t + 1) * 128]
+
+        @pl.loop(half * 16, half * 16 + 16, unroll=4)
+        def _(q):
+            base = pl.multiple_of(q * 32, 32)
+            lbuf[mine, q, 0:32, :] = t2[pl.ds(base, 32), :].astype(BF)
+            lbuf[mine, q, 32:64, :] = t2[pl.ds(1024 + base, 32), :].astype(BF)
+            low = t2[pl.ds(2048 + base, 16), :]
+            high = pltpu.roll(t2[pl.ds(2048 + base + 16, 16), :], 64, 1)
+            lbuf[mine, q, 64:80, :] = jnp.where(lane16 < 64, low, high).astype(BF)
 
     A, B = (0, 16), (16, 16)
-    CU, CD = (0, 8), (8, 8)
+    AU, AD, BU, BD = (0, 8), (8, 8), (16, 8), (24, 8)
 
     def part(x_, z_, c_, piece):
         return lbuf.at[slot(x_, z_, c_), pl.ds(piece[0], piece[1])]
 
+    def z_piece(direction, n, k):
+        if n < 3:
+            return B if k == 1 else A
+        return ((BU, BD) if k == 1 else (AU, AD))[direction]
+
     def z_copy(direction, n, k):
         origin = (z + 8 - n) % 8 if direction == 0 else (z + n) % 8
-        if k == 2:
-            piece = A if n < 3 else (CU if direction == 0 else CD)
-            ref = part(1 - x, origin, c, piece)
-        else:
-            ref = part(x, origin, c, (A, B)[k])
+        ref = part(1 - x if k == 2 else x, origin, c, z_piece(direction, n, k))
         return pltpu.make_async_remote_copy(
             src_ref=ref, dst_ref=ref, send_sem=zs.at[direction, n, k], recv_sem=zr.at[direction, n, k],
             device_id=up if direction == 0 else down, device_id_type=MESH)
 
     def z_arrival(direction, n, k):
         origin = (z + 8 - (n + 1)) % 8 if direction == 0 else (z + n + 1) % 8
-        if k == 2:
-            piece = A if n < 3 else (CU if direction == 0 else CD)
-            ref = part(1 - x, origin, c, piece)
-        else:
-            ref = part(x, origin, c, (A, B)[k])
+        ref = part(1 - x if k == 2 else x, origin, c, z_piece(direction, n, k))
         return pltpu.make_async_remote_copy(
             src_ref=ref, dst_ref=ref, send_sem=zs.at[direction, n, k], recv_sem=zr.at[direction, n, k],
             device_id=up if direction == 0 else down, device_id_type=MESH)
@@ -162,47 +160,46 @@
         copy.start()
         sent.append(copy)
 
-    def c_pieces(side, o):
-        if side == 1 and o == 4:
-            return [(CU, 0), (CD, 2), (B, 1)]
+    def c_pieces(o):
+        if o == 4:
+            return [(AU, 0), (AD, 2), (BU, 1), (BD, 3)]
         return [(A, 0), (B, 1)]
 
     def serve(n, k):
         for direction in (0, 1):
-            if n == 3 and k == (1 if direction == 0 else 0):
-                continue
             z_arrival(direction, n, k).wait_recv()
-            if n < 2 or (n == 2 and not k == (1 if direction == 0 else 0)):
+            if n < 3:
                 go(z_copy(direction, n + 1, k))
             o = (8 - (n + 1)) % 8 if direction == 0 else n + 1
-            if k == 0:
-                go(c_copy(0, o, A, 0))
-            elif k == 1:
-                go(x_copy(o, B, o))
-                go(c_copy(0, o, B, 1))
-            elif n < 3:
-                go(c_copy(1, o, A, 0))
-            else:
-                go(c_copy(1, o, CU if direction == 0 else CD, 0 if direction == 0 else 2))
+            piece = z_piece(direction, n, k)
+            second = 2 if n == 3 and direction == 1 else 0
+            if k == 1:
+                go(x_copy(o, piece, 9 if second else o))
+            go(c_copy(1 if k == 2 else 0, o, piece, second + (1 if k == 1 else 0)))
 
     def serve_x(o):
-        x_arrival(o, B, o).wait_recv()
-        go(c_copy(1, o, B, 1))
+        for piece, k in c_pieces(o):
+            if k % 2 == 1:
+                x_arrival(o, piece, 9 if k == 3 else o).wait_recv()
+                go(c_copy(1, o, piece, k))
 
     def have(o, half):
         for side in (0, 1):
-            for piece, k in c_pieces(side, o):
-                if (k == 1) == (half == 1):
+            for piece, k in c_pieces(o):
+                if k % 2 == half:
                     c_arrival(side, o, piece, k).wait_recv()
 
+    left_half(1)
+    pl.semaphore_wait(barrier, 8)
+    for direction in (0, 1):
+        go(z_copy(direction, 0, 1))
+    go(c_copy(0, 0, B, 1))
+    left_half(0)
     go(x_copy(0, A, 8))
     for direction in (0, 1):
         go(z_copy(direction, 0, 0))
-    for direction in (0, 1):
-        go(z_copy(direction, 0, 1))
     go(x_copy(0, B, 0))
     go(c_copy(0, 0, A, 0))
-    go(c_copy(0, 0, B, 1))
 
     rbuf[:, 0, 320:384, :] = jnp.zeros((32, 64, 256), BF)
     rbuf[:, 1, 256:320, :] = jnp.zeros((32, 64, 256), BF)
@@ -243,13 +240,15 @@
     for direction in (0, 1):
         go(z_copy(direction, 0, 2))
     go(c_copy(1, 0, A, 0))
-    right_steps(4, 8)
+    serve(0, 1)
+    right_steps(4, 9)
+    serve_x(0)
     serve(0, 0)
-    right_steps(8, 12)
-    serve_x(0)
-    right_steps(12, 16)
+    right_steps(9, 13)
+    serve_x(1)
+    serve_x(7)
     serve(0, 2)
-    serve(0, 1)
+    right_steps(13, 16)
     right_steps(16, 20, True)
 
     def contract(chips, half):
@@ -282,17 +281,41 @@
         target = cx * 2 + cz // 4
         rel = (y + 4 - target) % 4
         octets = pl.ds(8 * half, 8)
-        return target, pltpu.make_async_remote_copy(
+        return target, rel, pltpu.make_async_remote_copy(
             src_ref=sbuf.at[cx * 8 + cz, octets], dst_ref=ybuf.at[rel, cz % 4, octets],
             send_sem=ys.at[cx * 8 + cz, half], recv_sem=yr.at[rel, cz % 4, half],
-            device_id=dev(target, xh, x, z, c), device_id_type=MESH)
+            device_id=dev((target + jnp.where(rel == 2, 1 + 2 * c, 0)) % 4, xh, x, z, c), device_id_type=MESH)
 
     def send_sums(cx, cz, half):
-        target, copy = y_copy(cx, cz, half)
-
-        @pl.when(target != y)
+        target, rel, copy = y_copy(cx, cz, half)
+
+        @pl.when((rel != 0) & (rel != 1 + 2 * c))
         def _():
             copy.start()
+
+    def y_come(rel, zi, half):
+        ref = ybuf.at[rel, zi, pl.ds(8 * half, 8)]
+        pltpu.make_async_remote_copy(
+            src_ref=ref, dst_ref=ref, send_sem=ys.at[0, half], recv_sem=yr.at[rel, zi, half],
+            device_id=twin, device_id_type=MESH).wait_recv()
+
+    def relay(offsets, half):
+        for o in offsets:
+            for cx in (0, 1):
+                cz = at(o)
+                target, rel, copy = y_copy(cx, cz, half)
+
+                @pl.when(rel == 1 + 2 * c)
+                def _():
+                    zi = cz % 4
+                    mid = cx * 8 + cz
+                    y_come(2, zi, half)
+
+                    @pl.loop(8 * half, 8 * half + 8, unroll=2)
+                    def _(k):
+                        sbuf[mid, k] = (sbuf[mid, k].astype(F32) + ybuf[2, zi, k].astype(F32)).astype(BF)
+
+                    copy.start()
 
     def group(offsets, half):
         for o in offsets:
@@ -304,7 +327,7 @@
 
     def total(zi, o):
         v = sbuf[(y // 2) * 8 + (y % 2) * 4 + zi, o].astype(F32)
-        for rel in (1, 2, 3):
+        for rel in (1, 3):
             v += ybuf[rel, zi, o].astype(F32)
         return v
 
@@ -322,12 +345,8 @@
 
             @pl.when(cz // 4 == y % 2)
             def _():
-                for rel in (1, 2, 3):
-                    octets = pl.ds(8 * half, 8)
-                    pltpu.make_async_remote_copy(
-                        src_ref=ybuf.at[rel, zi, octets], dst_ref=ybuf.at[rel, zi, octets],
-                        send_sem=ys.at[0, half], recv_sem=yr.at[rel, zi, half],
-                        device_id=twin, device_id_type=MESH).wait_recv()
+                for rel in (1, 3):
+                    y_come(rel, zi, half)
 
                 @pl.when(zi // 2 == xh)
                 def _():
@@ -379,41 +398,49 @@
 
     gain_col = jnp.broadcast_to(out_gain[...], (128, 128)).T
 
+    group([0], 1)
     group([0], 0)
-    group([0], 1)
+    serve(1, 1)
+    relay([0], 1)
+    relay([0], 0)
+    group([1, 7], 1)
     serve(1, 0)
     group([1, 7], 0)
-    collect([0], 0)
-    serve_x(1)
-    serve_x(7)
     serve(1, 2)
-    group([1, 7], 1)
-    collect([0], 1)
-    serve(1, 1)
-    make_gates()
-    serve(2, 0)
-    group([2, 6], 0)
-    collect([1, 7], 0)
+    relay([1, 7], 1)
     serve_x(2)
     serve_x(6)
+    relay([1, 7], 0)
+    collect([0], 1)
+    collect([0], 0)
+    group([2, 6], 1)
+    serve(2, 1)
+    group([2, 6], 0)
+    serve(2, 0)
+    make_gates()
+    relay([2, 6], 1)
+    relay([2, 6], 0)
+    collect([1, 7], 1)
+    collect([1, 7], 0)
     serve(2, 2)
-    group([2, 6], 1)
-    collect([1, 7], 1)
-    serve(2, 1)
-    serve(3, 0)
-    group([3, 5], 0)
     serve_x(3)
     serve_x(5)
+    group([3, 5], 1)
     serve(3, 1)
-    group([3, 5], 1)
+    group([3, 5], 0)
+    relay([3, 5], 1)
+    collect([2, 6], 1)
+    serve(3, 0)
+    serve(3, 2)
+    relay([3, 5], 0)
+    serve_x(4)
+    group([4], 0)
+    group([4], 1)
     collect([2, 6], 0)
-    serve(3, 2)
-    group([4], 0)
-    serve_x(4)
-    group([4], 1)
-    collect([2, 6], 1)
+    relay([4], 0)
+    relay([4], 1)
+    collect([3, 5], 1)
     collect([3, 5], 0)
-    collect([3, 5], 1)
 
     place = (z + 8 - ((y % 2) * 4 + xh * 2)) % 8
     far = jnp.where((place >= 1) & (place <= 4), 0, 1)
@@ -429,7 +456,7 @@
             h_copy(zz, half).wait_send()
         for cx in (0, 1):
             for o in range(8):
-                target, copy = y_copy(cx, at(o), half)
+                target, rel, copy = y_copy(cx, at(o), half)
 
                 @pl.when(target != y)
                 def _():
@@ -464,8 +491,8 @@
             pltpu.VMEM((32, 80, 128), F32),
             dma, dma((2,)), dma((4,)),
             dma((2, 4, 3)), dma((2, 4, 3)),
-            dma((9,)), dma((9,)),
-            dma((2, 8, 3)), dma((2, 8, 3)),
+            dma((10,)), dma((10,)),
+            dma((2, 8, 4)), dma((2, 8, 4)),
             dma((16, 2)), dma((4, 4, 2)),
             dma((2, 2)), dma((2, 2)),
         ],

time: 146 us -> 132 us (0.904)
  Pallas kernels: 144 us -> 129 us
    pallas_call x1, Pallas kernels: 144 us -> 129 us  [step(): pl.pallas_call(kernel, out_shape=jax.ShapeDtypeStruct((32, 80, 128), BF),...]
where the time goes in v3:
time: 132 us; the launch traced here: 131 us
  Pallas kernels  129 us (98%)
  local copies, waits for them, and re-layouts  1.97 us (1%)
    pallas_call x1, Pallas kernels, step(): pl.pallas_call(kernel, out_shape=jax.ShapeDtypeStruct((32, 80, 128), BF),...  129 us

profile of v3, /device:TPU:160, one launch (start us, length us, event | category | flops | bytes accessed | tf_op | source)
XLA Modules:
  0.0 130.7 jit_solution(2833389206106454133)
XLA Ops:
  0.0 128.7 %triangle.1 = bf16[32,80,128]{2,1,0:T(8,128)(2,1)} custom-call(bf16[320,80,128]{2,1,0:T(8,128)(2,1)} %pair.1, f32[1,128]{1,0:T(1,128)} %bitcast.2, bf16[128,256]{1,0:T(8,128)(2,1)} %a_w.1, bf16[128,256]{1,0:T(8,128)(2,1)} %b_w.1, bf16[128,128]{1,0:T(8,128)(2,1)} %g_w.1, f32[1,128]{1,0:T(1,128)} %bitcast.3, bf16[128,128]{1,0:T(8,128)(2,1)} %o_w.1), custom_call_target="tpu_custom_call" | custom-call | tf_op jit(solution)/shard_map/triangle/pallas_call | solution.py:469
  128.7 2.0 %copy.9 = bf16[32,80,128]{2,1,0:T(8,128)(2,1)} copy(bf16[32,80,128]{2,1,0:T(8,128)(2,1)} %triangle.1) | data formatting | bytes 1310720

commit v4 on v3

--- a/solution.py
+++ b/solution.py
@@ -252,7 +252,7 @@
     right_steps(16, 20, True)
 
     def contract(chips, half):
-        @pl.loop(8 * half, 8 * half + 8)
+        @pl.loop(8 * half, 8 * half + 8, unroll=2)
         def _(o):
             tails = [[None, None] for _ in chips]
             for m in range(4):

time: 132 us -> 130 us (0.985)
  Pallas kernels: 129 us -> 127 us
    pallas_call x1, Pallas kernels: 129 us -> 127 us  [step(): pl.pallas_call(kernel, out_shape=jax.ShapeDtypeStruct((32, 80, 128), BF),...]
where the time goes in v4:
time: 130 us; the launch traced here: 129 us
  Pallas kernels  127 us (98%)
  local copies, waits for them, and re-layouts  1.97 us (2%)
    pallas_call x1, Pallas kernels, step(): pl.pallas_call(kernel, out_shape=jax.ShapeDtypeStruct((32, 80, 128), BF),...  127 us

profile of v4, /device:TPU:160, one launch (start us, length us, event | category | flops | bytes accessed | tf_op | source)
XLA Modules:
  0.0 128.6 jit_solution(18231159194383367410)
XLA Ops:
  0.0 126.6 %triangle.1 = bf16[32,80,128]{2,1,0:T(8,128)(2,1)} custom-call(bf16[320,80,128]{2,1,0:T(8,128)(2,1)} %pair.1, f32[1,128]{1,0:T(1,128)} %bitcast.2, bf16[128,256]{1,0:T(8,128)(2,1)} %a_w.1, bf16[128,256]{1,0:T(8,128)(2,1)} %b_w.1, bf16[128,128]{1,0:T(8,128)(2,1)} %g_w.1, f32[1,128]{1,0:T(1,128)} %bitcast.3, bf16[128,128]{1,0:T(8,128)(2,1)} %o_w.1), custom_call_target="tpu_custom_call" | custom-call | tf_op jit(solution)/shard_map/triangle/pallas_call | solution.py:469
  126.6 2.0 %copy.9 = bf16[32,80,128]{2,1,0:T(8,128)(2,1)} copy(bf16[32,80,128]{2,1,0:T(8,128)(2,1)} %triangle.1) | data formatting | bytes 1310720
